TPU v7x, 512 devices: a whole 4x8x8 slice. The times are simulated.
512 devices in a mesh: dom: 32 (over z, x), tm: 16 (over y, core).
Axes of the slice: x: 4, y: 8, z: 8, core: 2. Of those that a mesh axis runs over, the one named last changes fastest.
Arguments:
- signal: bfloat16 [8, 512, 65536], P(None, 'tm', 'dom'), may hold values from -6 to 6
- weights: bfloat16 [512, 5, 128, 128], P('dom'), may hold values from 0 to 10.5, as said below
- send_list: int32 [32, 4, 3], P('dom'), may hold values from 0 to 15, as said below
- col_ref: int32 [512, 5], P('dom'), may hold values from 0 to 27, as said below
- kernel: bfloat16 [512, 512], P('tm'), may hold values from -0.2 to 1.6
- cheb_coef: float32 [3], replicated, may hold values from 0.5 to 1.5
Outputs:
- filtered: bfloat16 [8, 512, 65536], P(None, 'tm', 'dom')
Inputs may be any that keep to these rules, and one draw needn't show every extreme that they name: `send_list`: for each q and k the 3 entries are distinct block rows of partition q. col_ref[g, 0] = g % 16. An entry e >= 16 of partition p names partition q = p + d_k (k = (e - 16) // 3), which always exists; for each p and k the slots s used run from 0 up to some count of at most 3, every such slot is used by some block row of p, and some partition uses all 3 from some k. `weights`: Nonnegative; every diagonal entry of slot 0 blocks is 0.5 or more.
All inputs are finite; a program needn't handle non-finite values.
Results may differ from a plain program's by a relative error of at most 0.023.
Values may be sent and summed in bfloat16 or wider, within the bound.
No kernel may reach another device: no remote copies, remote signals or barrier semaphores. Data moves between devices by JAX's collectives and lax.ppermute only.
A program may use at most 64 MiB of HBM per device.

v0:
```python
import jax
import jax.numpy as jnp
from jax import lax
from jax.sharding import PartitionSpec as P

REACH = 2


def from_behind(block, axis, distance):
    devices = range(lax.axis_size(axis))
    route = [(i - distance, i) for i in devices if i - distance in devices]
    return lax.ppermute(block, axis, route)


def body(signal, weights, send_list, col_ref, kernel, cheb_coef):
    probes, t_loc, n_loc = signal.shape
    blocks_here = weights.shape[0]
    block_size = weights.shape[2]
    row_count = probes * t_loc
    degree = jnp.sum(weights, axis=(1, 3), dtype=jnp.float32)
    inv_root = lax.rsqrt(degree)[:, None, :]
    signal_blocks = signal.reshape(row_count, blocks_here, block_size).transpose(1, 0, 2)
    offsets = list(range(-REACH, 0)) + list(range(1, REACH + 1))
    send_rows = send_list[0]

    def neighbour_product(field):
        scaled = (field.astype(jnp.float32) * inv_root).astype(jnp.bfloat16)
        received = []
        for way_index, distance in enumerate(offsets):
            outgoing = jnp.take(scaled, send_rows[way_index], axis=0)
            received.append(from_behind(outgoing, "dom", -distance))
        source = jnp.concatenate([scaled] + received, axis=0)
        picked = jnp.take(source, col_ref, axis=0)
        return jnp.einsum("bjrm,bjnm->brn", picked, weights, preferred_element_type=jnp.float32)

    first_sum = neighbour_product(signal_blocks)
    term_one = (-inv_root * first_sum).astype(jnp.bfloat16)
    second_sum = neighbour_product(term_one)
    term_two = (-2.0 * inv_root * second_sum - signal_blocks.astype(jnp.float32)).astype(
        jnp.bfloat16
    )
    combined_field = (
        cheb_coef[0] * signal_blocks.astype(jnp.float32)
        + cheb_coef[1] * term_one.astype(jnp.float32)
        + cheb_coef[2] * term_two.astype(jnp.float32)
    ).astype(jnp.bfloat16)
    time_whole = lax.all_to_all(
        combined_field.transpose(1, 0, 2).reshape(probes, t_loc, n_loc),
        "tm",
        split_axis=2,
        concat_axis=1,
        tiled=True,
    )
    filtered_whole = jnp.einsum(
        "ut,ptn->pun",
        lax.all_gather(kernel, "tm", axis=0, tiled=True),
        time_whole,
        preferred_element_type=jnp.float32,
    ).astype(jnp.bfloat16)
    return lax.all_to_all(filtered_whole, "tm", split_axis=1, concat_axis=2, tiled=True)


def solution(mesh):
    in_specs = (
        P(None, "tm", "dom"),
        P("dom", None, None, None),
        P("dom", None, None),
        P("dom", None),
        P("tm", None),
        P(),
    )
    out_specs = P(None, "tm", "dom")
    return jax.shard_map(body, mesh=mesh, in_specs=in_specs, out_specs=out_specs, check_vma=False)
```

profile of v0, /device:TPU:135, one launch (start us, length us, event | category | flops | bytes accessed | tf_op | source)
XLA Modules:
  0.0 193.9 jit_solution(8609952959684335362)
XLA Ops:
  0.0 1.2 slice_reduce_fusion
  1.2 2.2 %convert_reduce_fusion = f32[16,128]{1,0:T(8,128)S(1)} fusion(bf16[16,5,128,128]{3,2,1,0:T(8,128)(2,1)} %param.11), kind=kLoop, calls=%fused_computation.14 | loop fusion | flops 2619392 | bytes 2629632 | tf_op jit(solution)/shard_map/reduce_sum | solution.py:20
  5.7 4.8 %collective-permute-start = (bf16[3,256,128]{2,1,0:T(8,128)(2,1)S(1)}, bf16[3,256,128]{2,1,0:T(8,128)(2,1)S(1)}, u32[]{:S(2)}, u32[]{:S(2)}) collective-permute-start(bf16[3,256,128]{2,1,0:T(8,128)(2,1)S(1)} %broadcast_select_fusion.7), channel_id=1, source_target_pairs={{0,32},{16,48},{32,64},{48,80},{64,96},{80,112},{96,128},{112,144}... | collective-permute-start | bytes 589832 | tf_op jit(solution)/shard_map/ppermute | solution.py:12
  12.0 3.7 %collective-permute-start.1 = (bf16[3,256,128]{2,1,0:T(8,128)(2,1)}, bf16[3,256,128]{2,1,0:T(8,128)(2,1)}, u32[]{:S(2)}, u32[]{:S(2)}) collective-permute-start(bf16[3,256,128]{2,1,0:T(8,128)(2,1)} %broadcast_select_fusion.5), channel_id=1, source_target_pairs={{0,16},{16,32},{32,48},{48,64},{64,80},{80,96},{96,112},{112,128},... | collective-permute-start | bytes 589832 | tf_op jit(solution)/shard_map/ppermute | solution.py:12
  17.1 1.9 collective-permute-start.2
  19.7 1.9 collective-permute-start.3
  22.7 1.0 constant_dynamic-update-slice_fusion.2
  23.6 2.9 %collective-permute-done.2 = bf16[3,256,128]{2,1,0:T(8,128)(2,1)} collective-permute-done((bf16[3,256,128]{2,1,0:T(8,128)(2,1)}, bf16[3,256,128]{2,1,0:T(8,128)(2,1)}, u32[]{:S(2)}, u32[]{:S(2)}) %collective-permute-start.2) | collective-permute-done | bytes 196640 | tf_op jit(solution)/shard_map/ppermute | solution.py:12
  26.6 1.0 constant_dynamic-update-slice_fusion.1
  27.5 2.8 %collective-permute-done.3 = bf16[3,256,128]{2,1,0:T(8,128)(2,1)S(1)} collective-permute-done((bf16[3,256,128]{2,1,0:T(8,128)(2,1)S(1)}, bf16[3,256,128]{2,1,0:T(8,128)(2,1)S(1)}, u32[]{:S(2)}, u32[]{:S(2)}) %collective-permute-start.3) | collective-permute-done | bytes 196640 | tf_op jit(solution)/shard_map/ppermute | solution.py:12
  30.3 5.7 %gather_fusion.4 = bf16[80,256,128]{2,1,0:T(8,128)(2,1)} fusion(bf16[28,256,128]{2,1,0:T(8,128)(2,1)S(1)} %constant_dynamic-update-slice_fusion, s32[1024]{0:T(1024)S(1)} %pad_clamp_fusion), kind=kCustom, calls=%fused_computation.1.clone | custom fusion | bytes 10486080 | tf_op jit(solution)/shard_map/jit(_take)/gather | solution.py:33
  36.0 6.2 %constant_dynamic-update-slice_fusion.9 = (bf16[28,256,128]{2,1,0:T(8,128)(2,1)S(1)}, bf16[16,256,128]{2,1,0:T(8,128)(2,1)}, bf16[16,256,128]{2,1,0:T(8,128)(2,1)}) fusion(f32[16,128]{1,0:T(8,128)S(1)} %get-tuple-element.17, bf16[16,5,128,128]{3,2,1,0:T(8,128)(2,1)} %param.11, bf16[16,5,256,128]{3,2,1,0:T(8,128)(2,1)} %bitcast.65, ...), kind=kOutput, calls=%fused_computation.53 | convolution fusion | flops 676331520 | bytes 11026512 | tf_op jit(solution)/shard_map/bjrm,bjnm->brn/dot_general | solution.py:34
  42.2 1.8 gather_fusion.5
  44.0 1.8 gather_fusion.6
  45.8 1.8 gather_fusion.7
  47.7 1.8 gather_fusion.8
  49.6 5.0 %collective-permute-start.4 = (bf16[3,256,128]{2,1,0:T(8,128)(2,1)S(1)}, bf16[3,256,128]{2,1,0:T(8,128)(2,1)S(1)}, u32[]{:S(2)}, u32[]{:S(2)}) collective-permute-start(bf16[3,256,128]{2,1,0:T(8,128)(2,1)S(1)} %broadcast_select_fusion.6), channel_id=1, source_target_pairs={{0,32},{16,48},{32,64},{48,80},{64,96},{80,112},{96,128},{112,144}... | collective-permute-start | bytes 589832 | tf_op jit(solution)/shard_map/ppermute | solution.py:12
  54.7 6.4 %collective-permute-start.5 = (bf16[3,256,128]{2,1,0:T(8,128)(2,1)S(1)}, bf16[3,256,128]{2,1,0:T(8,128)(2,1)S(1)}, u32[]{:S(2)}, u32[]{:S(2)}) collective-permute-start(bf16[3,256,128]{2,1,0:T(8,128)(2,1)S(1)} %broadcast_select_fusion.4), channel_id=1, source_target_pairs={{0,16},{16,32},{32,48},{48,64},{64,80},{80,96},{96,112},{112,128},... | collective-permute-start | bytes 589832 | tf_op jit(solution)/shard_map/ppermute | solution.py:12
  61.1 1.9 collective-permute-start.6
  63.2 2.1 %collective-permute-start.7 = (bf16[3,256,128]{2,1,0:T(8,128)(2,1)S(1)}, bf16[3,256,128]{2,1,0:T(8,128)(2,1)S(1)}, u32[]{:S(2)}, u32[]{:S(2)}) collective-permute-start(bf16[3,256,128]{2,1,0:T(8,128)(2,1)S(1)} %broadcast_select_fusion), channel_id=1, source_target_pairs={{32,0},{48,16},{64,32},{80,48},{96,64},{112,80},{128,96},{144,112}... | collective-permute-start | bytes 589832 | tf_op jit(solution)/shard_map/ppermute | solution.py:12
  65.4 4.3 %collective-permute-done.6 = bf16[3,256,128]{2,1,0:T(8,128)(2,1)S(1)} collective-permute-done((bf16[3,256,128]{2,1,0:T(8,128)(2,1)S(1)}, bf16[3,256,128]{2,1,0:T(8,128)(2,1)S(1)}, u32[]{:S(2)}, u32[]{:S(2)}) %collective-permute-start.6) | collective-permute-done | bytes 196640 | tf_op jit(solution)/shard_map/ppermute | solution.py:12
  69.7 2.9 %collective-permute-done.7 = bf16[3,256,128]{2,1,0:T(8,128)(2,1)S(1)} collective-permute-done((bf16[3,256,128]{2,1,0:T(8,128)(2,1)S(1)}, bf16[3,256,128]{2,1,0:T(8,128)(2,1)S(1)}, u32[]{:S(2)}, u32[]{:S(2)}) %collective-permute-start.7) | collective-permute-done | bytes 196640 | tf_op jit(solution)/shard_map/ppermute | solution.py:12
  72.6 5.7 %gather_fusion.9 = bf16[80,256,128]{2,1,0:T(8,128)(2,1)} fusion(bf16[28,256,128]{2,1,0:T(8,128)(2,1)S(1)} %constant_dynamic-update-slice_fusion.5, s32[1024]{0:T(1024)S(1)} %pad_clamp_fusion), kind=kCustom, calls=%fused_computation.9.clone | custom fusion | bytes 10486080 | tf_op jit(solution)/shard_map/jit(_take)/gather | solution.py:33
  78.2 8.2 %fusion.11 = bf16[256,16,128]{2,0,1:T(8,128)(2,1)S(1)} fusion(bf16[16,256,128]{2,1,0:T(8,128)(2,1)} %get-tuple-element.21, f32[256,16,128]{2,1,0:T(8,128)} %bitcast.63, bf16[16,5,128,128]{3,2,1,0:T(8,128)(2,1)} %param.11, bf16[16,5,256,128]{3,2,1,0:T(8,128)(2,1)} %bitcast.64, pred[16,5]{1,0:T(8,128)(4,1)S(1)} %copy.36, ...), kind=kOutput, calls=%fused_computation.24 | convolution fusion | flops 679477248 | bytes 12066908 | tf_op jit(solution)/shard_map/bjrm,bjnm->brn/dot_general | solution.py:34
  87.0 3.4 %reshape.158 = bf16[8,32,2048]{1,0,2:T(8,128)(2,1)} reshape(bf16[256,16,128]{0,2,1:T(8,128)(2,1)S(1)} %copy.53) | data formatting | bytes 2097152 | tf_op jit(solution)/shard_map/reshape | solution.py:48
  90.4 7.4 %reshape.163 = bf16[16,2,16384]{2,1,0:T(2,128)(2,1)} reshape(bf16[2048,8,32]{2,1,0:T(8,128)(2,1)} %bitcast.60) | data formatting | bytes 2097152
  97.8 11.5 %all-to-all-start = ((bf16[16,2,16384]{2,1,0:T(2,128)(2,1)}), bf16[16,2,16384]{2,1,0:T(2,128)(2,1)S(1)}, u32[]{:S(2)}, u32[]{:S(2)}) async-start(bf16[16,2,16384]{2,1,0:T(2,128)(2,1)} %reshape.163), calls=%async_computation | async-start | bytes 2097152 | tf_op jit(solution)/shard_map/all_to_all | solution.py:47
  109.4 38.6 %all_gather.3 = bf16[512,512]{1,0:T(8,128)(2,1)S(1)} all-gather(bf16[32,512]{1,0:T(8,128)(2,1)S(1)} %copy-done.2), channel_id=1, replica_groups=mesh['dom'=32,'tm'=16] {'tm'}, dimensions={0}, use_global_device_ids=true | all-gather | bytes 557056 | tf_op jit(solution)/shard_map/all_gather | solution.py:56
  148.0 3.5 %reshape.164 = bf16[2048,8,32]{2,1,0:T(8,128)(2,1)} reshape(bf16[16,2,16384]{2,1,0:T(2,128)(2,1)S(1)} %all-to-all-done) | data formatting | bytes 2097152
  151.5 4.5 %copy.45 = bf16[8,16,32,128]{3,2,1,0:T(8,128)(2,1)S(1)} copy(bf16[8,16,32,128]{2,0,3,1:T(8,128)(2,1)} %bitcast.61) | data formatting | bytes 2097152 | tf_op jit(solution)/shard_map/all_to_all | solution.py:47
  157.6 34.3 %all_to_all.36 = bf16[8,512,128]{2,0,1:T(8,128)(2,1)S(1)} all-to-all(bf16[8,512,128]{2,0,1:T(8,128)(2,1)S(1)} %copy.47), channel_id=1, replica_groups=mesh['dom'=32,'tm'=16] {'tm'}, dimensions={1} | all-to-all | bytes 2097152 | tf_op jit(solution)/shard_map/all_to_all | solution.py:60
  192.6 1.3 all_to_all.33
  (57 shorter events, 9.9 us)
Async XLA Ops:
  0.0 3.4 %copy-start.1 = (bf16[8,32,2048]{2,1,0:T(8,128)(2,1)S(1)}, bf16[8,32,2048]{2,1,0:T(8,128)(2,1)}, u32[]{:S(2)}) copy-start(bf16[8,32,2048]{2,1,0:T(8,128)(2,1)} %param.10) | copy-start | bytes 3145732
  3.7 1.4 copy-start
  5.1 16.6 %copy-start.3 = (s32[16,5]{0,1:T(8,128)S(1)}, s32[16,5]{0,1:T(8,128)}, u32[]{:S(2)}) copy-start(s32[16,5]{0,1:T(8,128)} %param.13) | copy-start | bytes 964
  5.1 16.9 %copy-start.4 = (f32[3]{0:T(128)S(1)}, f32[3]{0:T(128)}, u32[]{:S(2)}) copy-start(f32[3]{0:T(128)} %param.15) | copy-start | bytes 40
  5.7 16.9 %collective-permute-start = (bf16[3,256,128]{2,1,0:T(8,128)(2,1)S(1)}, bf16[3,256,128]{2,1,0:T(8,128)(2,1)S(1)}, u32[]{:S(2)}, u32[]{:S(2)}) collective-permute-start(bf16[3,256,128]{2,1,0:T(8,128)(2,1)S(1)} %broadcast_select_fusion.7), channel_id=1, source_target_pairs={{0,32},{16,48},{32,64},{48,80},{64,96},{80,112},{96,128},{112,144}... | collective-permute-start | bytes 589832 | tf_op jit(solution)/shard_map/ppermute | solution.py:12
  12.0 10.7 %collective-permute-start.1 = (bf16[3,256,128]{2,1,0:T(8,128)(2,1)}, bf16[3,256,128]{2,1,0:T(8,128)(2,1)}, u32[]{:S(2)}, u32[]{:S(2)}) collective-permute-start(bf16[3,256,128]{2,1,0:T(8,128)(2,1)} %broadcast_select_fusion.5), channel_id=1, source_target_pairs={{0,16},{16,32},{32,48},{48,64},{64,80},{80,96},{96,112},{112,128},... | collective-permute-start | bytes 589832 | tf_op jit(solution)/shard_map/ppermute | solution.py:12
  17.1 9.5 %collective-permute-start.2 = (bf16[3,256,128]{2,1,0:T(8,128)(2,1)}, bf16[3,256,128]{2,1,0:T(8,128)(2,1)}, u32[]{:S(2)}, u32[]{:S(2)}) collective-permute-start(bf16[3,256,128]{2,1,0:T(8,128)(2,1)} %broadcast_select_fusion.3), channel_id=1, source_target_pairs={{16,0},{32,16},{48,32},{64,48},{80,64},{96,80},{112,96},{128,112},... | collective-permute-start | bytes 589832 | tf_op jit(solution)/shard_map/ppermute | solution.py:12
  19.7 10.6 %collective-permute-start.3 = (bf16[3,256,128]{2,1,0:T(8,128)(2,1)S(1)}, bf16[3,256,128]{2,1,0:T(8,128)(2,1)S(1)}, u32[]{:S(2)}, u32[]{:S(2)}) collective-permute-start(bf16[3,256,128]{2,1,0:T(8,128)(2,1)S(1)} %broadcast_select_fusion.1), channel_id=1, source_target_pairs={{32,0},{48,16},{64,32},{80,48},{96,64},{112,80},{128,96},{144,112}... | collective-permute-start | bytes 589832 | tf_op jit(solution)/shard_map/ppermute | solution.py:12
  49.6 15.7 %collective-permute-start.4 = (bf16[3,256,128]{2,1,0:T(8,128)(2,1)S(1)}, bf16[3,256,128]{2,1,0:T(8,128)(2,1)S(1)}, u32[]{:S(2)}, u32[]{:S(2)}) collective-permute-start(bf16[3,256,128]{2,1,0:T(8,128)(2,1)S(1)} %broadcast_select_fusion.6), channel_id=1, source_target_pairs={{0,32},{16,48},{32,64},{48,80},{64,96},{80,112},{96,128},{112,144}... | collective-permute-start | bytes 589832 | tf_op jit(solution)/shard_map/ppermute | solution.py:12
  54.7 10.7 %collective-permute-start.5 = (bf16[3,256,128]{2,1,0:T(8,128)(2,1)S(1)}, bf16[3,256,128]{2,1,0:T(8,128)(2,1)S(1)}, u32[]{:S(2)}, u32[]{:S(2)}) collective-permute-start(bf16[3,256,128]{2,1,0:T(8,128)(2,1)S(1)} %broadcast_select_fusion.4), channel_id=1, source_target_pairs={{0,16},{16,32},{32,48},{48,64},{64,80},{80,96},{96,112},{112,128},... | collective-permute-start | bytes 589832 | tf_op jit(solution)/shard_map/ppermute | solution.py:12
  61.1 8.5 %collective-permute-start.6 = (bf16[3,256,128]{2,1,0:T(8,128)(2,1)S(1)}, bf16[3,256,128]{2,1,0:T(8,128)(2,1)S(1)}, u32[]{:S(2)}, u32[]{:S(2)}) collective-permute-start(bf16[3,256,128]{2,1,0:T(8,128)(2,1)S(1)} %broadcast_select_fusion.2), channel_id=1, source_target_pairs={{16,0},{32,16},{48,32},{64,48},{80,64},{96,80},{112,96},{128,112},... | collective-permute-start | bytes 589832 | tf_op jit(solution)/shard_map/ppermute | solution.py:12
  63.2 9.4 %collective-permute-start.7 = (bf16[3,256,128]{2,1,0:T(8,128)(2,1)S(1)}, bf16[3,256,128]{2,1,0:T(8,128)(2,1)S(1)}, u32[]{:S(2)}, u32[]{:S(2)}) collective-permute-start(bf16[3,256,128]{2,1,0:T(8,128)(2,1)S(1)} %broadcast_select_fusion), channel_id=1, source_target_pairs={{32,0},{48,16},{64,32},{80,48},{96,64},{112,80},{128,96},{144,112}... | collective-permute-start | bytes 589832 | tf_op jit(solution)/shard_map/ppermute | solution.py:12
  97.8 11.5 %copy-start.2 = (bf16[32,512]{1,0:T(8,128)(2,1)S(1)}, bf16[32,512]{1,0:T(8,128)(2,1)}, u32[]{:S(2)}) copy-start(bf16[32,512]{1,0:T(8,128)(2,1)} %param.14) | copy-start | bytes 98308
  97.8 50.2 %all-to-all-start = ((bf16[16,2,16384]{2,1,0:T(2,128)(2,1)}), bf16[16,2,16384]{2,1,0:T(2,128)(2,1)S(1)}, u32[]{:S(2)}, u32[]{:S(2)}) async-start(bf16[16,2,16384]{2,1,0:T(2,128)(2,1)} %reshape.163), calls=%async_computation | async-start | bytes 2097152 | tf_op jit(solution)/shard_map/all_to_all | solution.py:47
where the time goes:
time: 195 us; the launch traced here: 194 us
  blocking collectives  73 us (37%)
  local copies, waits for them, and re-layouts  47.9 us (25%)
  starting transfers between devices  39.3 us (20%)
  matrix products  15.2 us (8%)
  waiting for transfers between devices  12.9 us (7%)
  other arithmetic  5.12 us (3%)
    all_gather x1, blocking collectives, body(): lax.all_gather(kernel, 'tm', axis=0, tiled=True)  38.6 us
    all_to_all x1, blocking collectives, body(): lax.all_to_all(filtered_whole, 'tm', split_axis=1, concat_axis=2, tiled=T...  34.3 us
    ppermute x8, starting transfers between devices, from_behind(): return lax.ppermute(block, axis, route)  27.8 us
    dot_general x2, matrix products, neighbour_product(): jnp.einsum('bjrm,bjnm->brn', picked, weights, preferred_element_type=jnp....  14.4 us
    unnamed x19, local copies, waits for them, and re-layouts  13.8 us
    ppermute x8, waiting for transfers between devices, from_behind(): return lax.ppermute(block, axis, route)  12.9 us
    all_to_all x1, starting transfers between devices, body(): lax.all_to_all(combined_field.transpose(1, 0, 2).reshape(probes, t_loc, n...  11.5 us
    gather x2, local copies, waits for them, and re-layouts, neighbour_product(): picked = jnp.take(source, col_ref, axis=0)  11.3 us
  transfers between devices with their start and end apart: 9, of which 4 were waited for; matrix products, arithmetic and copies ran while one was open for 3% of the time, Pallas kernels for 0%

commit v1 on v0

--- a/solution.py
+++ b/solution.py
@@ -44,12 +44,20 @@
         + cheb_coef[1] * term_one.astype(jnp.float32)
         + cheb_coef[2] * term_two.astype(jnp.float32)
     ).astype(jnp.bfloat16)
-    time_whole = lax.all_to_all(
-        combined_field.transpose(1, 0, 2).reshape(probes, t_loc, n_loc),
-        "tm",
-        split_axis=2,
-        concat_axis=1,
-        tiled=True,
+    time_whole = jnp.concatenate(
+        lax.all_to_all(
+            jnp.stack(
+                jnp.split(
+                    combined_field.transpose(1, 0, 2).reshape(probes, t_loc, n_loc),
+                    lax.axis_size("tm"),
+                    axis=2,
+                )
+            ),
+            "tm",
+            0,
+            0,
+        ),
+        axis=1,
     )
     filtered_whole = jnp.einsum(
         "ut,ptn->pun",

time: 195 us -> 187 us (0.959)
  local copies, waits for them, and re-layouts: 47.9 us -> 40.2 us
    all_to_all x1 -> x0, local copies, waits for them, and re-layouts: 4.52 us -> none  [body(): lax.all_to_all(combined_field.transpose(1, 0, 2).reshape(probes, t_loc, n...]
    reshape x2 -> x1, local copies, waits for them, and re-layouts: 3.89 us -> 0.49 us  [body(): combined_field.transpose(1, 0, 2).reshape(probes, t_loc, n_loc)]
    unnamed x19 -> x32, local copies, waits for them, and re-layouts: 13.8 us -> 12.5 us
  transfers between devices with their start and end apart: 9 -> 9, of which waited for: 4 -> 4; matrix products, arithmetic and copies ran while one was open for 3% -> 4% of each run, Pallas kernels for 0% -> 0%
where the time goes in v1:
time: 187 us; the launch traced here: 186 us
  blocking collectives  73 us (39%)
  local copies, waits for them, and re-layouts  40.2 us (21%)
  starting transfers between devices  39 us (21%)
  matrix products  15.2 us (8%)
  waiting for transfers between devices  13.1 us (7%)
  other arithmetic  5.12 us (3%)
    all_gather x1, blocking collectives, body(): lax.all_gather(kernel, 'tm', axis=0, tiled=True)  38.6 us
    all_to_all x1, blocking collectives, body(): lax.all_to_all(filtered_whole, 'tm', split_axis=1, concat_axis=2, tiled=T...  34.3 us
    ppermute x8, starting transfers between devices, from_behind(): return lax.ppermute(block, axis, route)  27.6 us
    dot_general x2, matrix products, neighbour_product(): jnp.einsum('bjrm,bjnm->brn', picked, weights, preferred_element_type=jnp....  14.4 us
    ppermute x8, waiting for transfers between devices, from_behind(): return lax.ppermute(block, axis, route)  13.1 us
    unnamed x32, local copies, waits for them, and re-layouts  12.5 us
    all_to_all x1, starting transfers between devices, body(): lax.all_to_all(jnp.stack(jnp.split(combined_field.transpose(1, 0, 2).resh...  11.4 us
    gather x2, local copies, waits for them, and re-layouts, neighbour_product(): picked = jnp.take(source, col_ref, axis=0)  11.3 us
  transfers between devices with their start and end apart: 9, of which 4 were waited for; matrix products, arithmetic and copies ran while one was open for 4% of the time, Pallas kernels for 0%

profile of v1, /device:TPU:135, one launch (start us, length us, event | category | flops | bytes accessed | tf_op | source)
XLA Modules:
  0.0 186.0 jit_solution(3094164349619691451)
XLA Ops:
  0.0 1.2 slice_reduce_fusion
  1.2 2.2 %convert_reduce_fusion = f32[16,128]{1,0:T(8,128)S(1)} fusion(bf16[16,5,128,128]{3,2,1,0:T(8,128)(2,1)} %param.11), kind=kLoop, calls=%fused_computation.14 | loop fusion | flops 2619392 | bytes 2629632 | tf_op jit(solution)/shard_map/reduce_sum | solution.py:20
  3.7 0.8 constant_dynamic-update-slice_fusion.4
  5.7 4.8 %collective-permute-start = (bf16[3,256,128]{2,1,0:T(8,128)(2,1)S(1)}, bf16[3,256,128]{2,1,0:T(8,128)(2,1)S(1)}, u32[]{:S(2)}, u32[]{:S(2)}) collective-permute-start(bf16[3,256,128]{2,1,0:T(8,128)(2,1)S(1)} %broadcast_select_fusion.7), channel_id=1, source_target_pairs={{0,32},{16,48},{32,64},{48,80},{64,96},{80,112},{96,128},{112,144}... | collective-permute-start | bytes 589832 | tf_op jit(solution)/shard_map/ppermute | solution.py:12
  11.2 0.8 broadcast_select_fusion.5
  12.0 3.7 %collective-permute-start.1 = (bf16[3,256,128]{2,1,0:T(8,128)(2,1)}, bf16[3,256,128]{2,1,0:T(8,128)(2,1)}, u32[]{:S(2)}, u32[]{:S(2)}) collective-permute-start(bf16[3,256,128]{2,1,0:T(8,128)(2,1)} %broadcast_select_fusion.5), channel_id=1, source_target_pairs={{0,16},{16,32},{32,48},{48,64},{64,80},{80,96},{96,112},{112,128},... | collective-permute-start | bytes 589832 | tf_op jit(solution)/shard_map/ppermute | solution.py:12
  16.3 0.8 broadcast_select_fusion.3
  17.1 1.9 %collective-permute-start.2 = (bf16[3,256,128]{2,1,0:T(8,128)(2,1)}, bf16[3,256,128]{2,1,0:T(8,128)(2,1)}, u32[]{:S(2)}, u32[]{:S(2)}) collective-permute-start(bf16[3,256,128]{2,1,0:T(8,128)(2,1)} %broadcast_select_fusion.3), channel_id=1, source_target_pairs={{16,0},{32,16},{48,32},{64,48},{80,64},{96,80},{112,96},{128,112},... | collective-permute-start | bytes 589832 | tf_op jit(solution)/shard_map/ppermute | solution.py:12
  19.7 1.9 %collective-permute-start.3 = (bf16[3,256,128]{2,1,0:T(8,128)(2,1)S(1)}, bf16[3,256,128]{2,1,0:T(8,128)(2,1)S(1)}, u32[]{:S(2)}, u32[]{:S(2)}) collective-permute-start(bf16[3,256,128]{2,1,0:T(8,128)(2,1)S(1)} %broadcast_select_fusion.1), channel_id=1, source_target_pairs={{32,0},{48,16},{64,32},{80,48},{96,64},{112,80},{128,96},{144,112}... | collective-permute-start | bytes 589832 | tf_op jit(solution)/shard_map/ppermute | solution.py:12
  22.7 1.0 constant_dynamic-update-slice_fusion.2
  23.6 2.9 %collective-permute-done.2 = bf16[3,256,128]{2,1,0:T(8,128)(2,1)} collective-permute-done((bf16[3,256,128]{2,1,0:T(8,128)(2,1)}, bf16[3,256,128]{2,1,0:T(8,128)(2,1)}, u32[]{:S(2)}, u32[]{:S(2)}) %collective-permute-start.2) | collective-permute-done | bytes 196640 | tf_op jit(solution)/shard_map/ppermute | solution.py:12
  26.6 1.0 constant_dynamic-update-slice_fusion.1
  27.5 2.8 %collective-permute-done.3 = bf16[3,256,128]{2,1,0:T(8,128)(2,1)S(1)} collective-permute-done((bf16[3,256,128]{2,1,0:T(8,128)(2,1)S(1)}, bf16[3,256,128]{2,1,0:T(8,128)(2,1)S(1)}, u32[]{:S(2)}, u32[]{:S(2)}) %collective-permute-start.3) | collective-permute-done | bytes 196640 | tf_op jit(solution)/shard_map/ppermute | solution.py:12
  30.3 5.7 %gather_fusion.4 = bf16[80,256,128]{2,1,0:T(8,128)(2,1)} fusion(bf16[28,256,128]{2,1,0:T(8,128)(2,1)S(1)} %constant_dynamic-update-slice_fusion, s32[1024]{0:T(1024)S(1)} %pad_clamp_fusion), kind=kCustom, calls=%fused_computation.1.clone | custom fusion | bytes 10486080 | tf_op jit(solution)/shard_map/jit(_take)/gather | solution.py:33
  36.0 6.2 %constant_dynamic-update-slice_fusion.9 = (bf16[28,256,128]{2,1,0:T(8,128)(2,1)S(1)}, bf16[16,256,128]{2,1,0:T(8,128)(2,1)}, bf16[16,256,128]{2,1,0:T(8,128)(2,1)}) fusion(f32[16,128]{1,0:T(8,128)S(1)} %get-tuple-element.17, bf16[16,5,128,128]{3,2,1,0:T(8,128)(2,1)} %param.11, bf16[16,5,256,128]{3,2,1,0:T(8,128)(2,1)} %bitcast.120, ...), kind=kOutput, calls=%fused_computation.85 | convolution fusion | flops 676331520 | bytes 11026512 | tf_op jit(solution)/shard_map/bjrm,bjnm->brn/dot_general | solution.py:34
  42.2 1.8 gather_fusion.5
  44.0 1.8 gather_fusion.6
  45.8 1.8 gather_fusion.7
  47.7 1.8 gather_fusion.8
  49.6 5.0 %collective-permute-start.4 = (bf16[3,256,128]{2,1,0:T(8,128)(2,1)S(1)}, bf16[3,256,128]{2,1,0:T(8,128)(2,1)S(1)}, u32[]{:S(2)}, u32[]{:S(2)}) collective-permute-start(bf16[3,256,128]{2,1,0:T(8,128)(2,1)S(1)} %broadcast_select_fusion.6), channel_id=1, source_target_pairs={{0,32},{16,48},{32,64},{48,80},{64,96},{80,112},{96,128},{112,144}... | collective-permute-start | bytes 589832 | tf_op jit(solution)/shard_map/ppermute | solution.py:12
  54.7 6.4 %collective-permute-start.5 = (bf16[3,256,128]{2,1,0:T(8,128)(2,1)S(1)}, bf16[3,256,128]{2,1,0:T(8,128)(2,1)S(1)}, u32[]{:S(2)}, u32[]{:S(2)}) collective-permute-start(bf16[3,256,128]{2,1,0:T(8,128)(2,1)S(1)} %broadcast_select_fusion.4), channel_id=1, source_target_pairs={{0,16},{16,32},{32,48},{48,64},{64,80},{80,96},{96,112},{112,128},... | collective-permute-start | bytes 589832 | tf_op jit(solution)/shard_map/ppermute | solution.py:12
  61.1 1.9 %collective-permute-start.6 = (bf16[3,256,128]{2,1,0:T(8,128)(2,1)S(1)}, bf16[3,256,128]{2,1,0:T(8,128)(2,1)S(1)}, u32[]{:S(2)}, u32[]{:S(2)}) collective-permute-start(bf16[3,256,128]{2,1,0:T(8,128)(2,1)S(1)} %broadcast_select_fusion.2), channel_id=1, source_target_pairs={{16,0},{32,16},{48,32},{64,48},{80,64},{96,80},{112,96},{128,112},... | collective-permute-start | bytes 589832 | tf_op jit(solution)/shard_map/ppermute | solution.py:12
  63.2 1.9 %collective-permute-start.7 = (bf16[3,256,128]{2,1,0:T(8,128)(2,1)S(1)}, bf16[3,256,128]{2,1,0:T(8,128)(2,1)S(1)}, u32[]{:S(2)}, u32[]{:S(2)}) collective-permute-start(bf16[3,256,128]{2,1,0:T(8,128)(2,1)S(1)} %broadcast_select_fusion), channel_id=1, source_target_pairs={{32,0},{48,16},{64,32},{80,48},{96,64},{112,80},{128,96},{144,112}... | collective-permute-start | bytes 589832 | tf_op jit(solution)/shard_map/ppermute | solution.py:12
  65.2 4.5 %collective-permute-done.6 = bf16[3,256,128]{2,1,0:T(8,128)(2,1)S(1)} collective-permute-done((bf16[3,256,128]{2,1,0:T(8,128)(2,1)S(1)}, bf16[3,256,128]{2,1,0:T(8,128)(2,1)S(1)}, u32[]{:S(2)}, u32[]{:S(2)}) %collective-permute-start.6) | collective-permute-done | bytes 196640 | tf_op jit(solution)/shard_map/ppermute | solution.py:12
  69.7 2.9 %collective-permute-done.7 = bf16[3,256,128]{2,1,0:T(8,128)(2,1)S(1)} collective-permute-done((bf16[3,256,128]{2,1,0:T(8,128)(2,1)S(1)}, bf16[3,256,128]{2,1,0:T(8,128)(2,1)S(1)}, u32[]{:S(2)}, u32[]{:S(2)}) %collective-permute-start.7) | collective-permute-done | bytes 196640 | tf_op jit(solution)/shard_map/ppermute | solution.py:12
  72.6 5.7 %gather_fusion.9 = bf16[80,256,128]{2,1,0:T(8,128)(2,1)} fusion(bf16[28,256,128]{2,1,0:T(8,128)(2,1)S(1)} %constant_dynamic-update-slice_fusion.5, s32[1024]{0:T(1024)S(1)} %pad_clamp_fusion), kind=kCustom, calls=%fused_computation.9.clone | custom fusion | bytes 10486080 | tf_op jit(solution)/shard_map/jit(_take)/gather | solution.py:33
  78.2 8.2 %fusion.11 = bf16[256,16,128]{2,0,1:T(8,128)(2,1)S(1)} fusion(bf16[16,256,128]{2,1,0:T(8,128)(2,1)} %get-tuple-element.21, f32[256,16,128]{2,1,0:T(8,128)} %bitcast.118, bf16[16,5,128,128]{3,2,1,0:T(8,128)(2,1)} %param.11, bf16[16,5,256,128]{3,2,1,0:T(8,128)(2,1)} %bitcast.119, pred[16,5]{1,0:T(8,128)(4,1)S(1)} %copy.51, ...), kind=kOutput, calls=%fused_computation.24 | convolution fusion | flops 679477248 | bytes 12066908 | tf_op jit(solution)/shard_map/bjrm,bjnm->brn/dot_general | solution.py:34
  98.0 11.4 %all-to-all-start = ((bf16[16,8,32,128]{3,2,1,0:T(8,128)(2,1)}), bf16[16,8,32,128]{3,2,1,0:T(8,128)(2,1)S(1)}, u32[]{:S(2)}, u32[]{:S(2)}) async-start(bf16[16,8,32,128]{3,2,1,0:T(8,128)(2,1)} %fusion.22), calls=%async_computation | async-start | bytes 2097152 | tf_op jit(solution)/shard_map/all_to_all | solution.py:48
  109.4 38.6 %all_gather.3 = bf16[512,512]{1,0:T(8,128)(2,1)S(1)} all-gather(bf16[32,512]{1,0:T(8,128)(2,1)S(1)} %copy-done.2), channel_id=1, replica_groups=mesh['dom'=32,'tm'=16] {'tm'}, dimensions={0}, use_global_device_ids=true | all-gather | bytes 557056 | tf_op jit(solution)/shard_map/all_gather | solution.py:64
  148.2 0.8 fusion.19
  149.7 34.3 %all_to_all.23 = bf16[8,512,128]{2,0,1:T(8,128)(2,1)S(1)} all-to-all(bf16[8,512,128]{2,0,1:T(8,128)(2,1)S(1)} %copy.60), channel_id=1, replica_groups=mesh['dom'=32,'tm'=16] {'tm'}, dimensions={1} | all-to-all | bytes 2097152 | tf_op jit(solution)/shard_map/all_to_all | solution.py:68
  184.7 1.3 all_to_all.20
  (71 shorter events, 17.9 us)
Async XLA Ops:
  0.0 3.4 %copy-start.1 = (bf16[8,32,2048]{2,1,0:T(8,128)(2,1)S(1)}, bf16[8,32,2048]{2,1,0:T(8,128)(2,1)}, u32[]{:S(2)}) copy-start(bf16[8,32,2048]{2,1,0:T(8,128)(2,1)} %param.10) | copy-start | bytes 3145732
  3.7 1.4 copy-start
  5.1 16.6 %copy-start.3 = (s32[16,5]{0,1:T(8,128)S(1)}, s32[16,5]{0,1:T(8,128)}, u32[]{:S(2)}) copy-start(s32[16,5]{0,1:T(8,128)} %param.13) | copy-start | bytes 964
  5.1 16.9 %copy-start.4 = (f32[3]{0:T(128)S(1)}, f32[3]{0:T(128)}, u32[]{:S(2)}) copy-start(f32[3]{0:T(128)} %param.15) | copy-start | bytes 40
  5.7 16.9 %collective-permute-start = (bf16[3,256,128]{2,1,0:T(8,128)(2,1)S(1)}, bf16[3,256,128]{2,1,0:T(8,128)(2,1)S(1)}, u32[]{:S(2)}, u32[]{:S(2)}) collective-permute-start(bf16[3,256,128]{2,1,0:T(8,128)(2,1)S(1)} %broadcast_select_fusion.7), channel_id=1, source_target_pairs={{0,32},{16,48},{32,64},{48,80},{64,96},{80,112},{96,128},{112,144}... | collective-permute-start | bytes 589832 | tf_op jit(solution)/shard_map/ppermute | solution.py:12
  12.0 10.7 %collective-permute-start.1 = (bf16[3,256,128]{2,1,0:T(8,128)(2,1)}, bf16[3,256,128]{2,1,0:T(8,128)(2,1)}, u32[]{:S(2)}, u32[]{:S(2)}) collective-permute-start(bf16[3,256,128]{2,1,0:T(8,128)(2,1)} %broadcast_select_fusion.5), channel_id=1, source_target_pairs={{0,16},{16,32},{32,48},{48,64},{64,80},{80,96},{96,112},{112,128},... | collective-permute-start | bytes 589832 | tf_op jit(solution)/shard_map/ppermute | solution.py:12
  17.1 9.5 %collective-permute-start.2 = (bf16[3,256,128]{2,1,0:T(8,128)(2,1)}, bf16[3,256,128]{2,1,0:T(8,128)(2,1)}, u32[]{:S(2)}, u32[]{:S(2)}) collective-permute-start(bf16[3,256,128]{2,1,0:T(8,128)(2,1)} %broadcast_select_fusion.3), channel_id=1, source_target_pairs={{16,0},{32,16},{48,32},{64,48},{80,64},{96,80},{112,96},{128,112},... | collective-permute-start | bytes 589832 | tf_op jit(solution)/shard_map/ppermute | solution.py:12
  19.7 10.6 %collective-permute-start.3 = (bf16[3,256,128]{2,1,0:T(8,128)(2,1)S(1)}, bf16[3,256,128]{2,1,0:T(8,128)(2,1)S(1)}, u32[]{:S(2)}, u32[]{:S(2)}) collective-permute-start(bf16[3,256,128]{2,1,0:T(8,128)(2,1)S(1)} %broadcast_select_fusion.1), channel_id=1, source_target_pairs={{32,0},{48,16},{64,32},{80,48},{96,64},{112,80},{128,96},{144,112}... | collective-permute-start | bytes 589832 | tf_op jit(solution)/shard_map/ppermute | solution.py:12
  49.6 15.5 %collective-permute-start.4 = (bf16[3,256,128]{2,1,0:T(8,128)(2,1)S(1)}, bf16[3,256,128]{2,1,0:T(8,128)(2,1)S(1)}, u32[]{:S(2)}, u32[]{:S(2)}) collective-permute-start(bf16[3,256,128]{2,1,0:T(8,128)(2,1)S(1)} %broadcast_select_fusion.6), channel_id=1, source_target_pairs={{0,32},{16,48},{32,64},{48,80},{64,96},{80,112},{96,128},{112,144}... | collective-permute-start | bytes 589832 | tf_op jit(solution)/shard_map/ppermute | solution.py:12
  54.7 10.5 %collective-permute-start.5 = (bf16[3,256,128]{2,1,0:T(8,128)(2,1)S(1)}, bf16[3,256,128]{2,1,0:T(8,128)(2,1)S(1)}, u32[]{:S(2)}, u32[]{:S(2)}) collective-permute-start(bf16[3,256,128]{2,1,0:T(8,128)(2,1)S(1)} %broadcast_select_fusion.4), channel_id=1, source_target_pairs={{0,16},{16,32},{32,48},{48,64},{64,80},{80,96},{96,112},{112,128},... | collective-permute-start | bytes 589832 | tf_op jit(solution)/shard_map/ppermute | solution.py:12
  61.1 8.5 %collective-permute-start.6 = (bf16[3,256,128]{2,1,0:T(8,128)(2,1)S(1)}, bf16[3,256,128]{2,1,0:T(8,128)(2,1)S(1)}, u32[]{:S(2)}, u32[]{:S(2)}) collective-permute-start(bf16[3,256,128]{2,1,0:T(8,128)(2,1)S(1)} %broadcast_select_fusion.2), channel_id=1, source_target_pairs={{16,0},{32,16},{48,32},{64,48},{80,64},{96,80},{112,96},{128,112},... | collective-permute-start | bytes 589832 | tf_op jit(solution)/shard_map/ppermute | solution.py:12
  63.2 9.4 %collective-permute-start.7 = (bf16[3,256,128]{2,1,0:T(8,128)(2,1)S(1)}, bf16[3,256,128]{2,1,0:T(8,128)(2,1)S(1)}, u32[]{:S(2)}, u32[]{:S(2)}) collective-permute-start(bf16[3,256,128]{2,1,0:T(8,128)(2,1)S(1)} %broadcast_select_fusion), channel_id=1, source_target_pairs={{32,0},{48,16},{64,32},{80,48},{96,64},{112,80},{128,96},{144,112}... | collective-permute-start | bytes 589832 | tf_op jit(solution)/shard_map/ppermute | solution.py:12
  87.7 21.8 %copy-start.2 = (bf16[32,512]{1,0:T(8,128)(2,1)S(1)}, bf16[32,512]{1,0:T(8,128)(2,1)}, u32[]{:S(2)}) copy-start(bf16[32,512]{1,0:T(8,128)(2,1)} %param.14) | copy-start | bytes 98308
  98.0 50.0 %all-to-all-start = ((bf16[16,8,32,128]{3,2,1,0:T(8,128)(2,1)}), bf16[16,8,32,128]{3,2,1,0:T(8,128)(2,1)S(1)}, u32[]{:S(2)}, u32[]{:S(2)}) async-start(bf16[16,8,32,128]{3,2,1,0:T(8,128)(2,1)} %fusion.22), calls=%async_computation | async-start | bytes 2097152 | tf_op jit(solution)/shard_map/all_to_all | solution.py:48
